TPU v7x, 32 devices: a whole 2x2x4 slice. The times are simulated.
32 devices in a mesh: dp: 8 (over y, x, core), expert: 4 (over z).
Axes of the slice: x: 2, y: 2, z: 4, core: 2. Of those that a mesh axis runs over, the one named last changes fastest.
Arguments:
- tokens: bfloat16 [32768, 1152], P(('dp', 'expert')), may hold values from -7 to 7
- norm_gain: float32 [1152], replicated, may hold values from 0.1 to 1.9
- router_weight: bfloat16 [1152, 4], replicated, may hold values from -1 to 1
- up_weight: bfloat16 [4, 1152, 3072], P('expert'), may hold values from -0.1875 to 0.1875
- down_weight: bfloat16 [4, 3072, 1152], P('expert'), may hold values from -0.625 to 0.625
- routes: int32 [32768, 1], P(('dp', 'expert')), may hold values from 0 to 3
- cotangent: bfloat16 [32768, 1152], P(('dp', 'expert')), may hold values from -6 to 6
Outputs:
- mixed: bfloat16 [32768, 1152], P(('dp', 'expert'))
- input_grad: float32 [32768, 1152], P(('dp', 'expert'))
- gain_grad: float32 [1152], replicated
- router_grad: float32 [1152, 4], replicated
- up_grad: float32 [4, 1152, 3072], P('expert', None, 'dp')
- down_grad: float32 [4, 3072, 1152], P('expert', 'dp')
All inputs are finite; a program needn't handle non-finite values.
Results may differ from a plain program's by a relative error of at most 0.0018.
The roundings to bfloat16 on the way count: a program that leaves them out, or rounds other values in their place, can miss the bound.
Values may be sent and summed in bfloat16 or wider, within the bound.
A program may use at most 192 MiB of HBM per device.

v0:
```python
import functools
import itertools

import jax
import jax.numpy as jnp
from jax import lax
from jax.experimental import pallas as pl
from jax.experimental.pallas import tpu as pltpu
from jax.sharding import PartitionSpec as P

ITERS = 8

norm_epsilon = 1e-06
root_half = 0.7071067811865476
inv_root_two_pi = 0.3989422804014327
f32 = jnp.float32
bf16 = jnp.bfloat16
MESH = pl.DeviceIdType.MESH
VMEM_BYTES = 60 * 1024 * 1024


def contract_last(left, right):
    return lax.dot_general(left, right, (((1,), (1,)), ((), ())), preferred_element_type=f32)


def contract_first(left, right):
    return lax.dot_general(left, right, (((0,), (0,)), ((), ())), preferred_element_type=f32)


def total_of(values):
    return jnp.sum(jnp.sum(values, axis=0, keepdims=True), axis=1, keepdims=True)


def at_least(value, multiple):
    return -(-value // multiple) * multiple


class Place:
    def __init__(self, planes, columns):
        self.planes, self.columns = planes, columns
        self.column = lax.axis_index("dp")
        self.plane = lax.axis_index("expert")
        self.index = self.column * planes + self.plane

    def plane_peer(self, k):
        peer, bit = 0, 1
        while bit < self.planes:
            here, there = lax.rem(lax.div(self.plane, bit), 2), lax.rem(lax.div(jnp.int32(k), bit), 2)
            peer = peer + bit * lax.rem(here + there, 2)
            bit *= 2
        return peer

    def order(self, i, sending):
        if self.planes != 4:
            return jnp.int32(i)
        outer, inner = ((1, 3, 2), (2, 3, 1)) if sending else ((2, 3, 1), (1, 3, 2))
        is_outer = jnp.logical_or(self.plane == 0, self.plane == self.planes - 1)
        made = jnp.int32(0)
        for at in range(3):
            k = jnp.where(is_outer, outer[at], inner[at])
            made = made + jnp.where(i == at + 1, k, 0)
        return made

    def column_peer(self, k):
        return lax.rem(self.column + k, self.columns)

    def enter(self):
        barrier = pltpu.get_barrier_semaphore()
        for k in range(1, self.planes):
            pl.semaphore_signal(barrier, inc=1, device_id=(self.column, self.plane_peer(k)), device_id_type=MESH)

        def greet(k, carry):
            pl.semaphore_signal(barrier, inc=1, device_id=(self.column_peer(k), self.plane), device_id_type=MESH)
            return carry

        lax.fori_loop(1, self.columns, greet, 0)
        pl.semaphore_wait(barrier, self.planes + self.columns - 2)


def remote(src, dst, send_sem, recv_sem, device):
    return pltpu.make_async_remote_copy(
        src_ref=src, dst_ref=dst, send_sem=send_sem, recv_sem=recv_sem, device_id=device, device_id_type=MESH
    )


def plane_gather(place, own, held, send, recv, begin=True):
    copies = []
    for k in range(1, place.planes):
        copy = remote(
            own, held.at[place.index], send.at[k], recv.at[k], (place.column, place.plane_peer(k))
        )
        if begin:
            copy.start()
        copies.append(copy)
    return copies


def column_copy(place, held, send, recv, k):
    mine = held.at[pl.ds(place.column * place.planes, place.planes)]
    return remote(mine, mine, send.at[k], recv.at[k], (place.column_peer(k), place.plane))


def column_gather_start(place, held, send, recv):
    def start(k, carry):
        column_copy(place, held, send, recv, k).start()
        return carry

    lax.fori_loop(1, place.columns, start, 0)


def column_gather_wait(place, held, send, recv):
    def wait(k, carry):
        column_copy(place, held, send, recv, k).wait()
        return carry

    lax.fori_loop(1, place.columns, wait, 0)


def balance_forward(target, logits_ref, probs_ref, rows_ref, scales_ref):
    blocks, experts = probs_ref.shape[:2]
    tile = logits_ref.shape[2:]
    zero = tuple(jnp.zeros(tile, f32) for _ in range(experts))

    def step_pass(step, first, scales):
        def block(n, sums):
            if first:
                held = [jnp.exp(logits_ref[n, e]) for e in range(experts)]
            else:
                held = [probs_ref[n, e] * scales[e] for e in range(experts)]
            row_total = sum(held[1:], held[0])
            rows_ref[step, n] = row_total
            after = [h / row_total for h in held]
            for e in range(experts):
                probs_ref[n, e] = after[e]
            return tuple(s + a for s, a in zip(sums, after))

        sums = lax.fori_loop(0, blocks, block, zero)
        made = [target / total_of(s) for s in sums]
        for e in range(experts):
            scales_ref[step, e] = jnp.broadcast_to(made[e], tile)
        return tuple(made)

    scales = step_pass(0, True, None)
    scales = lax.fori_loop(1, ITERS, lambda step, held: step_pass(step, False, held), scales)

    def last(n, carry):
        for e in range(experts):
            probs_ref[n, e] = probs_ref[n, e] * scales[e]
        return carry

    lax.fori_loop(0, blocks, last, 0)


def balance_backward(target, probs_ref, rows_ref, scales_ref, grads_ref):
    blocks, experts = probs_ref.shape[:2]
    zero = tuple(jnp.zeros(probs_ref.shape[2:], f32) for _ in range(experts))

    def first(n, dots):
        return tuple(dots[e] + probs_ref[n, e] * grads_ref[n, e] for e in range(experts))

    def step_pass(back, dots):
        step = ITERS - 1 - back
        means = [total_of(d) / target for d in dots]
        scales = [scales_ref[step, e] for e in range(experts)]
        inverse = [1.0 / s for s in scales]

        def block(n, dots):
            row_total = rows_ref[step, n]
            grads = [scales[e] * (grads_ref[n, e] - means[e]) for e in range(experts)]
            held = [probs_ref[n, e] * inverse[e] for e in range(experts)]
            terms = [g * h for g, h in zip(grads, held)]
            row_dot = sum(terms[1:], terms[0])
            made = []
            for e in range(experts):
                grad = (grads[e] - row_dot) / row_total
                before = held[e] * row_total
                grads_ref[n, e] = grad
                probs_ref[n, e] = before
                made.append(dots[e] + grad * before)
            return tuple(made)

        return lax.fori_loop(0, blocks, block, zero)

    lax.fori_loop(0, ITERS, step_pass, lax.fori_loop(0, blocks, first, zero))


def to_row(tile_ref, row_ref, row):
    tile = tile_ref[...]
    lanes = tile.shape[1]
    for k in range(tile.shape[0]):
        row_ref[row : row + 1, k * lanes : (k + 1) * lanes] = tile[k : k + 1, :]


def dispatch_kernel(
    planes, columns, capacity, base, choices,
    tokens, gain_in, router_in, routes, cotangent_in,
    landed, rows_out, grads_out, cot_rows, slots, notes, start_probs, probs, rows, scales, choice, router,
    normed, cotangent, sending, staging, all_logits, own_logits, row_buf,
    plane_send, plane_recv, column_send, column_recv, x_send, x_recv, x_local, local,
):
    place = Place(planes, columns)
    count, width = tokens.shape
    block = 128
    lanes = count // 8
    target = float(count * columns)
    load = pltpu.make_async_copy(cotangent_in, cotangent, local.at[1 + 2 * planes])
    load.start()
    gain = gain_in[...].reshape(1, width)
    router[...] = jnp.zeros_like(router)
    router[:planes, :] = router_in[...]

    def norm_block(i, carry):
        here = pl.ds(pl.multiple_of(i * block, block), block)
        values = tokens[here, :].astype(f32)
        inv_rms = lax.rsqrt(jnp.mean(values * values, axis=1, keepdims=True) + norm_epsilon)
        normed[here, :] = (values * inv_rms * gain).astype(bf16)
        return carry

    lax.fori_loop(0, count // block, norm_block, 0)
    row_buf[...] = contract_last(router[...], normed[...])
    route_row = routes[...]
    labels = lax.broadcasted_iota(jnp.int32, (router.shape[0], count), 0)
    chosen = jnp.where(labels == route_row, 1.0, 0.0)
    own_logits[planes] = jnp.broadcast_to(jnp.sum(chosen, axis=1, keepdims=True)[:8], own_logits.shape[1:])
    for e in range(planes):
        for k in range(8):
            own_logits[e, k : k + 1, :] = row_buf[e : e + 1, k * lanes : (k + 1) * lanes]
    all_logits[place.index] = own_logits[...]
    place.enter()
    gathers = plane_gather(place, own_logits, all_logits, plane_send, plane_recv)

    earlier = jnp.where(
        lax.broadcasted_iota(jnp.int32, (count, count), 0) < lax.broadcasted_iota(jnp.int32, (count, count), 1),
        1.0,
        0.0,
    ).astype(bf16)
    before = jnp.dot(chosen.astype(bf16), earlier, preferred_element_type=f32)
    position = jnp.sum(before * chosen, axis=0, keepdims=True)
    kept = position < capacity
    for e in range(planes):
        slots[e] = jnp.where(jnp.logical_and(kept, route_row == e), position, -1.0).astype(jnp.int32)
    notes[...] = jnp.zeros_like(notes)
    notes[1:2, :] = jnp.where(kept, route_row.astype(f32) * capacity + position, -1.0)

    def picked(e):
        return lax.broadcasted_iota(jnp.int32, (capacity, count), 0) == slots[e]

    copies, keeps = [], []
    first, later = pl.ds(0, base), pl.ds(base, capacity - base)
    for i in list(range(1, planes)) + [0]:
        k = place.order(i, True)
        e = place.plane_peer(k)
        onehot = jnp.where(picked(e), 1.0, 0.0).astype(bf16)
        sending[i] = jnp.dot(onehot, normed[...], preferred_element_type=f32).astype(bf16)
        if i:
            copy = remote(
                sending.at[i, first], landed.at[place.plane, first], x_send.at[k], x_recv.at[k], (place.column, e)
            )
            if base < capacity:
                keep = pltpu.make_async_copy(sending.at[i, later], rows_out.at[e, later], x_local.at[i])
                keep.start()
                keeps.append(keep)
        else:
            copy = pltpu.make_async_copy(sending.at[0], landed.at[place.plane], local.at[0])
        copy.start()
        copies.append(copy)
    for copy in gathers:
        copy.wait()
    column_gather_start(place, all_logits, column_send, column_recv)
    column_gather_wait(place, all_logits, column_send, column_recv)

    most = lax.fori_loop(
        1, planes * columns, lambda n, held: jnp.maximum(held, all_logits[n, planes]), all_logits[0, planes]
    )
    picks = jnp.full((1, most.shape[1]), len(choices) - 1, jnp.int32)
    for i in reversed(range(len(choices))):
        others = [most[e : e + 1, :] for e in range(planes) if e not in choices[i]]
        for other in others[1:]:
            others[0] = jnp.maximum(others[0], other)
        if others:
            picks = jnp.where(others[0] <= base, i, picks)
    choice[0] = picks[0, 0]

    balance_forward(target, all_logits, probs, rows, scales)
    start_probs[...] = jnp.exp(own_logits[:planes])
    gate = jnp.zeros((1, count), f32)
    for e in range(planes):
        to_row(probs.at[place.index, e], row_buf, e)
        gate = gate + jnp.where(route_row == e, row_buf[e : e + 1, :], 0.0)
    notes[0:1, :] = gate

    load.wait()
    for e in range(planes):
        if e >= 2:
            for copy in (copies[planes + 2 * (e - 2)], copies[planes + 2 * (e - 2) + 1]):
                copy.wait()
        slot = e % 2
        mask = picked(e)
        slot_gate = jnp.sum(jnp.where(mask, gate, 0.0), axis=1, keepdims=True)
        onehot = jnp.where(mask, 1.0, 0.0).astype(bf16)
        moved = jnp.dot(onehot, cotangent[...], preferred_element_type=f32)
        staging[slot, 0] = moved.astype(bf16)
        staging[slot, 1] = (slot_gate * moved).astype(bf16)
        for i, out in enumerate((cot_rows, grads_out)):
            copy = pltpu.make_async_copy(staging.at[slot, i], out.at[e], local.at[1 + 2 * e + i])
            copy.start()
            copies.append(copy)
    for copy in keeps + copies[:planes] + copies[planes + 2 * (planes - 2) :]:
        copy.wait()


def gelu_parts(values):
    return 0.5 * (1.0 + lax.erf(values * root_half))


def expert_kernel(
    planes, columns, capacity, base, count, heavy,
    up, down, landed, rows_out, grads_out, cot_rows, slots, notes, start_probs, probs, rows, scales,
    tokens, cotangent, gain_in, router,
    back_stage, slope_stage, back_landed, slope_landed, pair_landed, sum_landed, all_grads,
    up_out, down_out, mixed_out, input_out, totals_out,
    x, g, sums_out, own_sum, own_grads, row_buf, blank, notes_out,
    router_part, router_own, router_planes, router_columns,
    x_send, x_recv, x_local, fill_sem, total_sem, total_column_sem, plane_send, plane_recv, column_send, column_recv, g_send, g_recv, back_send, back_recv, slope_send, slope_recv,
    pair_send, pair_recv, sum_send, sum_recv, local, stage_sem, mixed_sem,
):
    place = Place(planes, columns)
    width, hidden = up.shape[1:]
    chips = columns // 2
    share = hidden // columns
    joint = 1
    while (joint * 2 * share) % 128:
        joint *= 2
    groups = chips // joint
    group_rows = joint * 2 * share
    core = lax.rem(place.column, 2)
    chip = lax.div(place.column, 2)
    my_group = lax.div(chip, joint)
    in_group = lax.rem(chip, joint)
    tile = 512
    tiles = hidden // tile
    peers = list(range(1, planes))

    column, plane = place.column, place.plane
    extra = capacity - base
    first, later = pl.ds(0, base), pl.ds(base, extra)
    light = [e for e in range(planes) if e not in heavy] if extra else []

    def taking(n):
        return place.order(n, False)

    def pieces(expert, run):
        run(0, first)
        if extra:
            if light:
                is_heavy = functools.reduce(jnp.logical_or, [expert == e for e in heavy])
                pl.when(is_heavy)(lambda: run(1, later))
            else:
                run(1, later)

    def later_piece(expert, run):
        pieces(expert, lambda i, where: run() if i else None)

    def x_copy(k):
        e = place.plane_peer(k)
        return remote(rows_out.at[e, later], x.at[plane, later], x_send.at[k], x_recv.at[k], (column, e))

    def g_copy(k, i, where):
        e = place.plane_peer(k)
        return remote(grads_out.at[e, where], g.at[plane, where], g_send.at[i, k], g_recv.at[i, k], (column, e))

    def plane_copy(stage, dst, send, recv, k, i, where):
        e = place.plane_peer(k)
        return remote(stage.at[e, where], dst.at[plane, where], send.at[i, k], recv.at[i, k], (column, e))

    def back_copy(*which):
        return plane_copy(back_stage, back_landed, back_send, back_recv, *which)

    def slope_copy(*which):
        return plane_copy(slope_stage, slope_landed, slope_send, slope_recv, *which)

    place.enter()
    for n in peers:
        k = place.order(n, True)
        later_piece(place.plane_peer(k), lambda: x_copy(k).start())
    for n in peers:
        k = place.order(n, True)
        pieces(place.plane_peer(k), lambda i, where: g_copy(k, i, where).start())
    own_g = pltpu.make_async_copy(grads_out.at[plane], g.at[plane], local.at[0])
    own_g.start()
    own_x = pltpu.make_async_copy(landed.at[plane], x.at[plane], x_local.at[0])
    own_x.start()

    def x_load(k):
        e = place.plane_peer(k)
        return pltpu.make_async_copy(landed.at[e, first], x.at[e, first], x_local.at[k])

    for k in peers:
        x_load(k).start()

    def fills(run):
        for e in light:
            @pl.when(plane != e)
            def _():
                for i, dst in enumerate((back_landed, slope_landed)):
                    run(pltpu.make_async_copy(blank, dst.at[e, later], fill_sem.at[i, e]))

    if light:
        blank[...] = jnp.zeros_like(blank)
        fills(lambda copy: copy.start())

        @pl.when(functools.reduce(jnp.logical_or, [plane == e for e in light]))
        def _():
            for k in peers:
                x[place.plane_peer(k), later, :] = jnp.zeros((extra, width), bf16)
                g[place.plane_peer(k), later, :] = jnp.zeros((extra, width), bf16)

    def part(kind, gi, u):
        group = lax.rem(my_group + 1 + gi, groups)
        inside = lax.rem(in_group + u, joint)
        return group * joint + inside, inside

    def sum_copy(kind, gi, u):
        there, _ = part(kind, gi, u)
        return remote(
            sums_out.at[kind, gi * joint + (u - 1) % joint], sum_landed.at[kind, chip],
            sum_send.at[kind, gi * joint + (u - 1) % joint], sum_recv.at[kind, chip], (there * 2 + core, place.plane),
        )

    def compute(act, pre_g):
        def experts(w_up, w_down, acc, out):
            load_up = pltpu.make_async_copy(up.at[0], w_up, local.at[2])
            load_down = pltpu.make_async_copy(down.at[0], w_down, local.at[3])
            load_up.start()
            load_down.start()
            own_x.wait()
            load_up.wait()
            load_down.wait()
            def put_copy(i, stage, s):
                slot = lax.rem(i, 2)
                return pltpu.make_async_copy(out.at[slot], stage.at[s], stage_sem.at[slot])

            def put(i, stage, landed_here, s):
                pl.when(i >= 2)(lambda: put_copy(i, stage, s).wait())
                out[lax.rem(i, 2)] = acc[...].astype(bf16)
                pl.when(i == 0)(lambda: put_copy(i, landed_here, s).start())
                pl.when(i > 0)(lambda: put_copy(i, stage, s).start())

            def finish_puts(stage):
                for i in range(2):
                    put_copy(i, stage, plane).wait()

            def forward(s):
                acc[...] = jnp.zeros_like(acc)

                def step(t, carry):
                    here = pl.ds(pl.multiple_of(t * tile, tile), tile)
                    pre = jnp.dot(x[s], w_up[:, here], preferred_element_type=f32)
                    made = (pre * gelu_parts(pre)).astype(bf16)
                    acc[...] += jnp.dot(made, w_down[here, :], preferred_element_type=f32)
                    return carry

                lax.fori_loop(0, tiles, step, 0)

            def backward(s):
                acc[...] = jnp.zeros_like(acc)

                def step(t, carry):
                    here = pl.ds(pl.multiple_of(t * tile, tile), tile)
                    pre = jnp.dot(x[s], w_up[:, here], preferred_element_type=f32)
                    act_g = contract_last(g[s], w_down[here, :])
                    half = gelu_parts(pre)
                    act[s, :, here] = (pre * half).astype(bf16)
                    slope = half + pre * jnp.exp(-0.5 * pre * pre) * inv_root_two_pi
                    made = (act_g * slope).astype(bf16)
                    pre_g[s, :, here] = made
                    acc[...] += contract_last(made, w_up[:, here])
                    return carry

                lax.fori_loop(0, tiles, step, 0)

            def send_backs():
                for j in peers:
                    pieces(place.plane_peer(j), lambda i, where: g_copy(j, i, where).wait_send())
                for m in peers:
                    j = place.order(m, True)
                    pieces(plane, lambda i, where: back_copy(j, i, where).start())

            def forward_step(n, carry):
                k = taking(n)

                @pl.when(n > 0)
                def _():
                    x_load(k).wait()
                    later_piece(plane, lambda: x_copy(k).wait_recv())

                s = place.plane_peer(k)
                forward(s)
                put(n, back_stage, back_landed, s)
                return carry

            lax.fori_loop(0, planes, forward_step, 0)
            finish_puts(back_stage)
            own_g.wait()

            def backward_step(n, carry):
                k = taking(n)

                @pl.when(n > 0)
                def _():
                    pieces(plane, lambda i, where: g_copy(k, i, where).wait_recv())

                s = place.plane_peer(k)
                backward(s)
                put(n, slope_stage, slope_landed, s)

                pl.when(n == 1)(send_backs)
                return carry

            lax.fori_loop(0, planes, backward_step, 0)
            finish_puts(slope_stage)

        pl.run_scoped(
            experts,
            pltpu.VMEM((width, hidden), bf16),
            pltpu.VMEM((hidden, width), bf16),
            pltpu.VMEM((capacity, width), f32),
            pltpu.VMEM((2, capacity, width), bf16),
        )

        def weight_sums(stage, other, back_rows, held_rows):
            piece = 384
            while group_rows % piece:
                piece -= 128
            across = 3 if width % 384 == 0 else 1
            breadth = width // across
            kinds = ((pre_g, x), (act, g))

            def form(kind, gi):
                left, right = kinds[kind]
                group = lax.rem(my_group + 1 + gi, groups)

                def step(i, carry):
                    t, c = lax.div(i, across), lax.rem(i, across)
                    rows_here = pl.ds(pl.multiple_of(t * piece, piece), piece)
                    lanes_here = pl.ds(pl.multiple_of(group * group_rows + t * piece, 128), piece)
                    cut = pl.ds(pl.multiple_of(c * breadth, 128), breadth)
                    stage[kind, rows_here, cut] = contract_first(
                        left[:, :, lanes_here].reshape(planes * capacity, piece),
                        right[:, :, cut].reshape(planes * capacity, breadth),
                    )
                    return carry

                lax.fori_loop(0, group_rows // piece * across, step, 0)

            def pair_copy(kind, gi, u):
                _, inside = part(kind, gi, u)
                theirs = pl.ds(pl.multiple_of((inside * 2 + 1 - core) * share, 8), share)
                return remote(
                    stage.at[kind, theirs], pair_landed.at[kind, gi, u],
                    pair_send.at[kind, gi, u], pair_recv.at[kind, gi, u], (place.column + 1 - 2 * core, place.plane),
                )

            def finish(kind, gi):
                for u in range(joint):
                    pair_copy(kind, gi, u).wait()
                    load = pltpu.make_async_copy(pair_landed.at[kind, gi, u], other, local.at[4])
                    load.start()
                    load.wait()
                    _, inside = part(kind, gi, u)
                    mine = pl.ds(pl.multiple_of((inside * 2 + core) * share, 8), share)

                    def pass_on():
                        sums_out[kind, gi * joint + (u - 1) % joint] = (stage[kind, mine, :] + other[...]).astype(bf16)
                        sum_copy(kind, gi, u).start()

                    def keep():
                        own_sum[kind] = stage[kind, mine, :] + other[...]

                    if u:
                        pass_on()
                    else:
                        pl.when(gi < groups - 1)(pass_on)
                        pl.when(gi == groups - 1)(keep)

            def group_step(j, carry):
                kind, gi = lax.rem(j, 2), lax.div(j, 2)
                pl.when(gi > 0)(lambda: finish(kind, gi - 1))

                @pl.when(gi < groups)
                def _():
                    pl.when(kind == 0)(lambda: form(0, gi))
                    pl.when(kind == 1)(lambda: form(1, gi))
                    for u in range(joint):
                        pair_copy(kind, gi, u).start()

                pl.when(j == 2 * groups - 3)(begin_slopes)

                @pl.when(j == 2 * groups - 1)
                def _():
                    gate_grads(back_rows, held_rows)
                    send_slopes()

                return carry

            lax.fori_loop(0, 2 * groups + 2, group_step, 0)

        return pl.run_scoped(
            weight_sums,
            pltpu.VMEM((2, group_rows, width), f32),
            pltpu.VMEM((share, width), f32),
            pltpu.VMEM((capacity, width), bf16),
            pltpu.VMEM((capacity, width), bf16),
        )

    own_grads_copy = pltpu.make_async_copy(own_grads, all_grads.at[place.index], local.at[10])

    def gate_grads(back_rows, held_rows):
        lanes = count // 8
        if light:
            fills(lambda copy: copy.wait())

        def dots_step(n, carry):
            k = taking(n)
            e = place.plane_peer(k)

            @pl.when(n > 0)
            def _():
                pieces(e, lambda i, where: back_copy(k, i, where).wait_recv())

            fetch = [
                pltpu.make_async_copy(src.at[e], dst, local.at[8 + i])
                for i, (src, dst) in enumerate(((back_landed, back_rows), (cot_rows, held_rows)))
            ]
            for copy in fetch:
                copy.start()
            for copy in fetch:
                copy.wait()
            dots = jnp.sum(back_rows[...].astype(f32) * held_rows[...].astype(f32), axis=1, keepdims=True)
            mask = lax.broadcasted_iota(jnp.int32, (capacity, count), 0) == slots[e]
            row_buf[0:1, :] = jnp.sum(jnp.where(mask, dots, 0.0), axis=0, keepdims=True)
            for i in range(8):
                own_grads[e, i : i + 1, :] = row_buf[0:1, i * lanes : (i + 1) * lanes]
            return carry

        lax.fori_loop(0, planes, dots_step, 0)
        own_grads_copy.start()
        plane_gather(place, own_grads, all_grads, plane_send, plane_recv)

    def begin_slopes():
        for k in peers:
            pieces(plane, lambda i, where: back_copy(k, i, where).wait_send())
        slope_copy(planes - 1, 0, first).start()

    def send_slopes():
        for n in peers:
            k = place.order(n, True)

            def start(i, where):
                if i:
                    slope_copy(k, i, where).start()
                else:
                    pl.when(k != planes - 1)(lambda: slope_copy(k, i, where).start())

            pieces(plane, start)

    pl.run_scoped(
        lambda act, pre_g: (compute(act, pre_g), None)[1],
        pltpu.VMEM((planes, capacity, hidden), bf16),
        pltpu.VMEM((planes, capacity, hidden), bf16),
    )

    block, long = 128, 256

    def place_of(i, size=block):
        return pl.ds(pl.multiple_of(i * size, size), size)

    def onehot_of(target, start, size):
        labels = lax.broadcasted_iota(jnp.int32, (target.shape[0], size), 1) + start
        return jnp.where(labels == target, 1.0, 0.0).astype(bf16)

    def mix_tokens(tok, back_rows, mixed_buf):
        loads = [
            pltpu.make_async_copy(src, dst, local.at[5 + i])
            for i, (src, dst) in enumerate(((tokens, tok), (back_landed, back_rows)))
        ]
        for load in loads:
            load.start()
        for load in loads:
            load.wait()

        def mixed_copy(i):
            return pltpu.make_async_copy(mixed_buf.at[i], mixed_out.at[place_of(i, long)], mixed_sem.at[i])

        def mix(i, carry):
            here = place_of(i, long)
            cols = notes[:, here].T
            onehot = onehot_of(cols[:, 1:2].astype(jnp.int32), 0, planes * capacity)
            returned = jnp.dot(onehot, back_rows[...].reshape(planes * capacity, width), preferred_element_type=f32)
            mixed_buf[i] = (tok[here, :].astype(f32) + cols[:, 0:1] * returned).astype(bf16)
            mixed_copy(i).start()
            return carry

        lax.fori_loop(0, count // long, mix, 0)
        for i in range(count // long):
            mixed_copy(i).wait()

    pl.run_scoped(
        mix_tokens,
        pltpu.VMEM((count, width), bf16),
        pltpu.VMEM((planes, capacity, width), bf16),
        pltpu.VMEM((count // long, long, width), bf16),
    )
    for copy in plane_gather(place, own_grads, all_grads, plane_send, plane_recv, False):
        copy.wait()
    own_grads_copy.wait()
    column_gather_start(place, all_grads, column_send, column_recv)

    def total_copy(part, held, sems, k):
        return remote(part, held.at[plane], sems.at[0, k], sems.at[1, k], (column, place.plane_peer(k)))

    def total_column_copy(own, held, sems, k):
        return remote(own, held.at[column], sems.at[0, k], sems.at[1, k], (place.column_peer(k), plane))

    def total_start(part, planes_held):
        planes_held[plane] = part[...]
        for k in peers:
            total_copy(part, planes_held, total_sem, k).start()

    def total_middle(part, planes_held, own, columns_held):
        for k in peers:
            total_copy(part, planes_held, total_sem, k).wait()
        own[...] = lax.fori_loop(1, planes, lambda e, held: held + planes_held[e], planes_held[0])
        columns_held[column] = own[...]

        def start(k, carry):
            total_column_copy(own, columns_held, total_column_sem, k).start()
            return carry

        lax.fori_loop(1, columns, start, 0)

    def total_end(own, columns_held, out):
        def wait(k, carry):
            total_column_copy(own, columns_held, total_column_sem, k).wait()
            return carry

        lax.fori_loop(1, columns, wait, 0)
        out[...] = lax.fori_loop(1, columns, lambda c, held: held + columns_held[c], columns_held[0])

    def route_grads(probs_here, rows_here, scales_here, grads_here):
        loads = [
            pltpu.make_async_copy(src, dst, local.at[5 + i])
            for i, (src, dst) in enumerate(((probs, probs_here), (rows, rows_here), (scales, scales_here)))
        ]
        for load in loads:
            load.start()
        column_gather_wait(place, all_grads, column_send, column_recv)
        fetch = pltpu.make_async_copy(all_grads, grads_here, local.at[11])
        fetch.start()
        fetch.wait()
        for load in loads:
            load.wait()
        balance_backward(float(count * columns), probs_here, rows_here, scales_here, grads_here)
        notes_out[...] = notes[...]
        for e in range(planes):
            own_grads[e] = grads_here[place.index, e] * start_probs[e]
            to_row(own_grads.at[e], notes_out, 2 + e)

    tile_shape = start_probs.shape
    devices = planes * columns
    def token_side(tok, cot, routed, slope_rows, grad_buf, part):
        loads = [
            pltpu.make_async_copy(src, dst, local.at[2 + i]) for i, (src, dst) in enumerate(((tokens, tok), (cotangent, cot)))
        ]
        for load in loads:
            load.start()
        routed[...] = jnp.zeros_like(routed)

        def fetch_rows(n):
            k = taking(n)
            e = place.plane_peer(k)

            @pl.when(n > 0)
            def _():
                pieces(e, lambda i, where: slope_copy(k, i, where).wait_recv())

            load = pltpu.make_async_copy(slope_landed.at[e], slope_rows, local.at[0])
            load.start()
            load.wait()
            return e

        def rows_at(e, here):
            target = notes[:, here].T[:, 1:2].astype(jnp.int32)
            return jnp.dot(onehot_of(target, e * capacity, capacity), slope_rows[...], preferred_element_type=f32)

        def chunk(n, carry):
            e = fetch_rows(n)

            def step(i, carry):
                here = place_of(i, long)
                routed[here, :] += rows_at(e, here)
                return carry

            return lax.fori_loop(0, count // long, step, carry)

        lax.fori_loop(0, planes - 1, chunk, 0)
        pl.run_scoped(
            route_grads,
            pltpu.VMEM((devices,) + tile_shape, f32),
            pltpu.VMEM((ITERS, devices) + tile_shape[1:], f32),
            pltpu.VMEM((ITERS,) + tile_shape, f32),
            pltpu.VMEM((devices,) + tile_shape, f32),
        )
        for load in loads:
            load.wait()
        gain = gain_in[...].reshape(1, width)
        e = fetch_rows(planes - 1)
        router_part[...] = jnp.zeros_like(router_part)

        def grad_copy(i):
            slot = lax.rem(i, 2)
            return pltpu.make_async_copy(grad_buf.at[slot], input_out.at[place_of(i)], stage_sem.at[slot])

        def last(i, gains):
            here = place_of(i)
            whole = notes_out[:, here]
            cols = whole.T
            values = tok[here, :].astype(f32)
            inv_rms = lax.rsqrt(jnp.mean(values * values, axis=1, keepdims=True) + norm_epsilon)
            unit = values * inv_rms
            through = cols[:, 2:3] * router[0:1, :].astype(f32)
            for c in range(1, planes):
                through = through + cols[:, 2 + c : 3 + c] * router[c : c + 1, :].astype(f32)
            normed_grad = routed[here, :] + rows_at(e, here) + through
            unit_grad = normed_grad * gain
            pl.when(i >= 2)(lambda: grad_copy(i).wait())
            grad_buf[lax.rem(i, 2)] = cot[here, :].astype(f32) + inv_rms * (
                unit_grad - unit * jnp.mean(unit_grad * unit, axis=1, keepdims=True)
            )
            grad_copy(i).start()
            normed = (unit * gain).astype(bf16)
            high = whole.astype(bf16)
            rest = whole - high.astype(f32)
            middle = rest.astype(bf16)
            low = (rest - middle.astype(f32)).astype(bf16)
            product = jnp.dot(high, normed, preferred_element_type=f32)
            product = product + jnp.dot(middle, normed, preferred_element_type=f32)
            router_part[...] += product + jnp.dot(low, normed, preferred_element_type=f32)
            return gains + jnp.sum(normed_grad * unit, axis=0, keepdims=True)

        gains = lax.fori_loop(0, count // block, last, jnp.zeros((1, width), f32))
        router_part[0:1, :] = gains
        total_start(router_part, router_planes)

        def part_load(j):
            kind, there = lax.rem(j, 2), lax.rem(chip + 1 + lax.div(j, 2), chips)
            return pltpu.make_async_copy(sum_landed.at[kind, there], part.at[lax.rem(j, 2)], local.at[3 + lax.rem(j, 2)])

        def part_arrived(j):
            kind, there = lax.rem(j, 2), lax.rem(chip + 1 + lax.div(j, 2), chips)
            remote(
                sums_out.at[kind, 0], sum_landed.at[kind, there],
                sum_send.at[kind, 0], sum_recv.at[kind, there], (there * 2 + core, plane),
            ).wait_recv()
            part_load(j).start()

        def add(j, carry):
            pl.when(j < 2 * chips - 3)(lambda: part_arrived(j + 1))
            part_load(j).wait()
            kind = lax.rem(j, 2)
            own_sum[kind] = own_sum[kind] + part[kind].astype(f32)
            return carry

        part_arrived(jnp.int32(0))
        lax.fori_loop(0, 2 * chips - 2, add, 0)
        sum_copies = [
            pltpu.make_async_copy(own_sum.at[kind], out, local.at[12 + kind])
            for kind, out in enumerate((up_out, down_out))
        ]
        for copy in sum_copies:
            copy.start()
        total_middle(router_part, router_planes, router_own, router_columns)
        for i in range(2):
            grad_copy(i).wait()
        for copy in sum_copies:
            copy.wait()
        total_end(router_own, router_columns, totals_out)

    pl.run_scoped(
        token_side,
        pltpu.VMEM((count, width), bf16),
        pltpu.VMEM((count, width), bf16),
        pltpu.VMEM((count, width), f32),
        pltpu.VMEM((capacity, width), bf16),
        pltpu.VMEM((2, block, width), f32),
        pltpu.VMEM((2, share, width), bf16),
    )

    def sent(j, carry):
        kind, i = lax.rem(j, 2), lax.div(j, 2)
        remote(
            sums_out.at[kind, i], sum_landed.at[kind, chip],
            sum_send.at[kind, i], sum_recv.at[kind, chip], (column, plane),
        ).wait_send()
        return carry

    lax.fori_loop(0, 2 * chips - 2, sent, 0)
    for k in peers:
        later_piece(place.plane_peer(k), lambda: x_copy(k).wait_send())
        pieces(plane, lambda i, where: slope_copy(k, i, where).wait_send())


def result_kernel(planes, up_in, down_in, mixed_in, input_in, totals, up, down, mixed, inputs, gain, router, rows, turned, wide, sem):
    half = inputs.shape[0] // 2
    moves = [
        (up_in, rows.at[0], None),
        (input_in.at[pl.ds(0, half)], wide.at[pl.ds(0, half)], inputs.at[pl.ds(0, half)]),
        (input_in.at[pl.ds(half, half)], wide.at[pl.ds(half, half)], inputs.at[pl.ds(half, half)]),
        (mixed_in, turned[1], mixed),
        (down_in, rows.at[1], down.at[0]),
    ]
    loads = [pltpu.make_async_copy(src, held, sem.at[0, i]) for i, (src, held, _) in enumerate(moves)]
    for load in loads:
        load.start()
    gain[...] = totals[0, :]
    router[...] = totals[2 : 2 + planes, :]
    stores = []
    for i, (_, held, dst) in enumerate(moves):
        loads[i].wait()
        if i == 0:
            turned[0][...] = rows[0].T
            held, dst = turned[0], up.at[0]
        store = pltpu.make_async_copy(held, dst, sem.at[1, i])
        store.start()
        stores.append(store)
    for store in stores:
        store.wait()


def call(kernel, outs, out_spaces, scratch, number, *arrays):
    spec = lambda space: pl.BlockSpec(memory_space=space)
    return pl.pallas_call(
        kernel,
        out_shape=[jax.ShapeDtypeStruct(shape, kind) for shape, kind in outs],
        in_specs=[spec(space) for _, space in arrays],
        out_specs=[spec(space) for space in out_spaces],
        scratch_shapes=scratch,
        compiler_params=pltpu.CompilerParams(
            collective_id=number, has_side_effects=True, vmem_limit_bytes=VMEM_BYTES
        ),
    )(*[array for array, _ in arrays])


def on_device(tokens, norm_gain, router_weight, up_weight, down_weight, routes, cotangent):
    count, width = tokens.shape
    planes = lax.axis_size("expert")
    columns = lax.axis_size("dp")
    devices = planes * columns
    capacity = 3 * count // (2 * planes)
    hidden = up_weight.shape[2]
    chips = columns // 2
    share = hidden // columns
    tile = (planes, 8, count // 8)
    tall = (planes + 1, 8, count // 8)
    note_rows = at_least(2 + planes, 8)
    vmem, hbm = pltpu.VMEM, pltpu.HBM
    dma = lambda *shape: pltpu.SemaphoreType.DMA(shape)

    base, choices = capacity, [()]
    if planes <= 4:
        base = at_least(capacity * 9 // 16, 16)
        half = planes // 2
        choices = list(itertools.product(range(half), range(half, planes))) + [tuple(range(planes))]
    extra = capacity - base

    slab = (planes, capacity, width)
    landed, rows_out, grads_out, cot_rows, slots, notes, start_probs, probs, rows, scales, choice, router = call(
        functools.partial(dispatch_kernel, planes, columns, capacity, base, choices),
        [
            (slab, bf16), (slab, bf16), (slab, bf16), (slab, bf16), ((planes, 1, count), jnp.int32), ((note_rows, count), f32),
            (tile, f32), ((devices,) + tile, f32), ((ITERS, devices) + tile[1:], f32), ((ITERS,) + tile, f32), ((1,), jnp.int32), ((16, width), bf16),
        ],
        [hbm, hbm, hbm, hbm, vmem, vmem, vmem, vmem, vmem, vmem, pltpu.SMEM, vmem],
        [
            pltpu.VMEM((count, width), bf16),
            pltpu.VMEM((count, width), bf16),
            pltpu.VMEM(slab, bf16),
            pltpu.VMEM((2, 2, capacity, width), bf16),
            pltpu.VMEM((devices,) + tall, f32),
            pltpu.VMEM(tall, f32),
            pltpu.VMEM((16, count), f32),
            dma(planes), dma(planes), dma(columns), dma(columns), dma(planes), dma(planes), dma(planes), dma(2 + 2 * planes),
        ],
        0,
        (tokens, vmem), (norm_gain, vmem), (router_weight.T, vmem), (routes.reshape(1, count), vmem), (cotangent, hbm),
    )

    joint = 1
    while (joint * 2 * share) % 128:
        joint *= 2
    groups = chips // joint
    def experts(number, heavy, *arrays):
        return call(
        functools.partial(expert_kernel, planes, columns, capacity, base, count, heavy),
        [
            (slab, bf16), (slab, bf16), (slab, bf16), (slab, bf16),
            ((2, groups, joint, share, width), f32), ((2, chips, share, width), bf16), ((devices,) + tile, f32),
            ((share, width), f32), ((share, width), f32), ((count, width), bf16), ((count, width), f32),
            ((note_rows, width), f32),
        ],
        [hbm] * 11 + [vmem],
        [
            pltpu.VMEM(slab, bf16),
            pltpu.VMEM(slab, bf16),
            pltpu.VMEM((2, chips, share, width), bf16),
            pltpu.VMEM((2, share, width), f32),
            pltpu.VMEM(tile, f32),
            pltpu.VMEM((8, count), f32),
            pltpu.VMEM((max(extra, 16), width), bf16),
            pltpu.VMEM((note_rows, count), f32),
            pltpu.VMEM((note_rows, width), f32),
            pltpu.VMEM((note_rows, width), f32),
            pltpu.VMEM((planes, note_rows, width), f32),
            pltpu.VMEM((columns, note_rows, width), f32),
            dma(planes), dma(planes), dma(planes), dma(2, planes), dma(2, planes), dma(2, columns), dma(planes), dma(planes), dma(columns), dma(columns),
            dma(2, planes), dma(2, planes), dma(2, planes), dma(2, planes), dma(2, planes), dma(2, planes),
            dma(2, groups, joint), dma(2, groups, joint), dma(2, chips), dma(2, chips), dma(14), dma(2), dma(count // 256),
        ],
        number,
        *zip(arrays, [hbm] * 6 + [vmem] * 3 + [hbm] * 5 + [vmem] * 2),
    )

    arrays = (
        up_weight, down_weight, landed, rows_out, grads_out, cot_rows, slots, notes, start_probs, probs, rows, scales,
        tokens, cotangent, norm_gain, router,
    )
    branches = [functools.partial(experts, 1 + i, heavy) for i, heavy in enumerate(choices)]
    outs = branches[0](*arrays) if len(branches) == 1 else lax.switch(choice[0], branches, *arrays)
    spec = lambda space: pl.BlockSpec(memory_space=space)
    up_grad, down_grad, mixed, input_grad, gain_grad, router_grad = pl.pallas_call(
        functools.partial(result_kernel, planes),
        out_shape=[
            jax.ShapeDtypeStruct((1, width, share), f32),
            jax.ShapeDtypeStruct((1, share, width), f32),
            jax.ShapeDtypeStruct((count, width), bf16),
            jax.ShapeDtypeStruct((count, width), f32),
            jax.ShapeDtypeStruct((width,), f32),
            jax.ShapeDtypeStruct((planes, width), f32),
        ],
        in_specs=[spec(hbm)] * 4 + [spec(vmem)],
        out_specs=[spec(hbm)] * 4 + [spec(vmem)] * 2,
        scratch_shapes=[
            pltpu.VMEM((2, share, width), f32),
            [pltpu.VMEM((width, share), f32), pltpu.VMEM((count, width), bf16)],
            pltpu.VMEM((count, width), f32),
            dma(2, 5),
        ],
        compiler_params=pltpu.CompilerParams(vmem_limit_bytes=VMEM_BYTES),
    )(*outs[7:])
    return mixed, input_grad, gain_grad, router_grad.T, up_grad, down_grad


def solution(mesh):
    in_specs = (
        P(("dp", "expert"), None),
        P(),
        P(),
        P("expert", None, None),
        P("expert", None, None),
        P(("dp", "expert"), None),
        P(("dp", "expert"), None),
    )
    out_specs = (
        P(("dp", "expert"), None),
        P(("dp", "expert"), None),
        P(),
        P(),
        P("expert", None, "dp"),
        P("expert", "dp", None),
    )
    return jax.shard_map(
        on_device, mesh=mesh, in_specs=in_specs, out_specs=out_specs, check_vma=False
    )
```

profile of v0, /device:TPU:0, one launch (start us, length us, event | category | flops | bytes accessed | tf_op | source)
XLA Modules:
  0.0 376.5 jit_solution(9280016069837484188)
XLA Ops:
  0.6 0.0 copy-start
  0.6 48.2 %shard_map.118 = (bf16[4,384,1152]{2,1,0:T(8,128)(2,1)S(1)}, bf16[4,384,1152]{2,1,0:T(8,128)(2,1)}, bf16[4,384,1152]{2,1,0:T(8,128)(2,1)}, bf16[4,384,1152]{2,1,...) custom-call(bf16[1024,1152]{1,0:T(8,128)(2,1)} %tokens.1, ...), custom_call_target="tpu_custom_call" | custom-call | tf_op jit(solution)/shard_map/pallas_call | solution.py:942
  49.4 0.0 copy-done
  49.5 317.3 %conditional.1 = (f32[384,1152]{1,0:T(8,128)}, f32[384,1152]{1,0:T(8,128)}, bf16[1024,1152]{1,0:T(8,128)(2,1)}, f32[1024,1152]{1,0:T(8,128)}, f32[8,1152]{1,0:T(8,128)}) conditional(s32[]{:T(128)} %bitcast.2, (bf16[1,1152,3072]{2,1,0:T(8,128)(2,1)}, bf16[1,3072,1152]{2,1,0:T(8,128)(2,1)}, ...), branch_computations={%region_0.0_spmd, %region_1.0_spmd, %region_2.0_spmd, %region_3.0_... | conditional | bytes 40 | solution.py:1038
  62.4 304.1 %branch_4_fun.1 = (bf16[4,384,1152]{2,1,0:T(8,128)(2,1)}, bf16[4,384,1152]{2,1,0:T(8,128)(2,1)}, bf16[4,384,1152]{2,1,0:T(8,128)(2,1)}, bf16[4,384,1152]{2,1,0:T...) custom-call(bf16[1,1152,3072]{2,1,0:T(8,128)(2,1)} %get-tuple-elemen, ...), custom_call_target="tpu_custom_call" | custom-call | tf_op jit(solution)/shard_map/cond/branch_4_fun/pallas_call | solution.py:942
  366.8 9.4 %shard_map.119 = (f32[1,1152,384]{2,1,0:T(8,128)}, f32[1,384,1152]{2,1,0:T(8,128)}, bf16[1024,1152]{1,0:T(8,128)(2,1)}, f32[1024,1152]{1,0:T(8,128)}, f32[1152]{0:T(1024)}, /*index=5*/f32[4,1152]{1,0:T(4,128)}) custom-call(f32[384,1152]{1,0:T(8,128)} %get-tuple-element.306.up_in, f32[384,1152]{1,0:T(8,128)} %get-tuple-element.307.down_in, ...), custom_call_target="tpu_custom_call" | custom-call | tf_op jit(solution)/shard_map/pallas_call | solution.py:1040
Async XLA Ops:
  0.6 48.8 %copy-start = (f32[1152]{0:T(1024)S(1)}, f32[1152]{0:T(1024)}, u32[]{:S(2)}) copy-start(f32[1152]{0:T(1024)} %gain_in.1) | copy-start | bytes 13828
where the time goes:
time: 369 us; the launch traced here: 376 us
  Pallas kernels  362 us (98%)
  loops' own time  13.3 us (4%)
    pallas_call x2, Pallas kernels, call(): pl.pallas_call(kernel, out_shape=[jax.ShapeDtypeStruct(shape, kind) for s...  352 us
    another operation x1, loops' own time, on_device(): lax.switch(choice[0], branches, *arrays)  13.3 us
    pallas_call x1, Pallas kernels, on_device(): pl.pallas_call(functools.partial(result_kernel, planes), out_shape=[jax.S...  9.38 us

commit v1 on v0

--- a/solution.py
+++ b/solution.py
@@ -83,16 +83,13 @@
     )
 
 
-def plane_gather(place, own, held, send, recv, begin=True):
-    copies = []
-    for k in range(1, place.planes):
-        copy = remote(
-            own, held.at[place.index], send.at[k], recv.at[k], (place.column, place.plane_peer(k))
-        )
-        if begin:
-            copy.start()
-        copies.append(copy)
-    return copies
+def plane_gather(place, own, held, send, recv, begin):
+    def step(k, carry):
+        copy = remote(own, held.at[place.index], send.at[k], recv.at[k], (place.column, place.plane_peer(k)))
+        copy.start() if begin else copy.wait()
+        return carry
+
+    lax.fori_loop(1, place.planes, step, 0)
 
 
 def column_copy(place, held, send, recv, k):
@@ -227,7 +224,7 @@
             own_logits[e, k : k + 1, :] = row_buf[e : e + 1, k * lanes : (k + 1) * lanes]
     all_logits[place.index] = own_logits[...]
     place.enter()
-    gathers = plane_gather(place, own_logits, all_logits, plane_send, plane_recv)
+    plane_gather(place, own_logits, all_logits, plane_send, plane_recv, True)
 
     earlier = jnp.where(
         lax.broadcasted_iota(jnp.int32, (count, count), 0) < lax.broadcasted_iota(jnp.int32, (count, count), 1),
@@ -264,8 +261,7 @@
             copy = pltpu.make_async_copy(sending.at[0], landed.at[place.plane], local.at[0])
         copy.start()
         copies.append(copy)
-    for copy in gathers:
-        copy.wait()
+    plane_gather(place, own_logits, all_logits, plane_send, plane_recv, False)
     column_gather_start(place, all_logits, column_send, column_recv)
     column_gather_wait(place, all_logits, column_send, column_recv)
 
@@ -307,6 +303,14 @@
             copies.append(copy)
     for copy in keeps + copies[:planes] + copies[planes + 2 * (planes - 2) :]:
         copy.wait()
+
+
+def by_rows(count, run, size=96):
+    def step(i, carry):
+        run(pl.ds(pl.multiple_of(i * size, size), size))
+        return carry
+
+    lax.fori_loop(0, count // size, step, 0)
 
 
 def gelu_parts(values):
@@ -352,18 +356,14 @@
     def pieces(expert, run):
         run(0, first)
         if extra:
-            if light:
-                is_heavy = functools.reduce(jnp.logical_or, [expert == e for e in heavy])
-                pl.when(is_heavy)(lambda: run(1, later))
-            else:
-                run(1, later)
+            pl.when(is_heavy(expert))(lambda: run(1, later))
 
     def later_piece(expert, run):
         pieces(expert, lambda i, where: run() if i else None)
 
-    def x_copy(k):
+    def x_copy(k, where):
         e = place.plane_peer(k)
-        return remote(rows_out.at[e, later], x.at[plane, later], x_send.at[k], x_recv.at[k], (column, e))
+        return remote(rows_out.at[e, where], x.at[plane, where], x_send.at[k], x_recv.at[k], (column, e))
 
     def g_copy(k, i, where):
         e = place.plane_peer(k)
@@ -379,13 +379,39 @@
     def slope_copy(*which):
         return plane_copy(slope_stage, slope_landed, slope_send, slope_recv, *which)
 
+    def each(run):
+        def step(n, carry):
+            run(place.order(n, True))
+            return carry
+
+        lax.fori_loop(1, planes, step, 0)
+
+    def is_heavy(expert):
+        return functools.reduce(jnp.logical_or, [expert == e for e in heavy]) if light else True
+
+    def spread(start, expert=None, wanted=None):
+        for i, (low, size) in enumerate(((0, base), (base, extra))):
+            part = size // 2 if light and size % 32 == 0 else max(size, 16)
+
+            def one(p, carry):
+                where = pl.ds(pl.multiple_of(low + p * part, 16), part)
+
+                def to(k):
+                    need = True
+                    if i:
+                        need = is_heavy(place.plane_peer(k) if expert is None else expert)
+                    if wanted is not None:
+                        need = jnp.logical_and(need, wanted(k, i))
+                    pl.when(need)(lambda: start(k, i, where))
+
+                each(to)
+                return carry
+
+            lax.fori_loop(0, size // part, one, 0)
+
     place.enter()
-    for n in peers:
-        k = place.order(n, True)
-        later_piece(place.plane_peer(k), lambda: x_copy(k).start())
-    for n in peers:
-        k = place.order(n, True)
-        pieces(place.plane_peer(k), lambda i, where: g_copy(k, i, where).start())
+    spread(lambda k, i, where: x_copy(k, where).start() if i else None)
+    spread(lambda k, i, where: g_copy(k, i, where).start())
     own_g = pltpu.make_async_copy(grads_out.at[plane], g.at[plane], local.at[0])
     own_g.start()
     own_x = pltpu.make_async_copy(landed.at[plane], x.at[plane], x_local.at[0])
@@ -395,8 +421,7 @@
         e = place.plane_peer(k)
         return pltpu.make_async_copy(landed.at[e, first], x.at[e, first], x_local.at[k])
 
-    for k in peers:
-        x_load(k).start()
+    each(lambda k: x_load(k).start())
 
     def fills(run):
         for e in light:
@@ -411,9 +436,11 @@
 
         @pl.when(functools.reduce(jnp.logical_or, [plane == e for e in light]))
         def _():
-            for k in peers:
+            def clear(k):
                 x[place.plane_peer(k), later, :] = jnp.zeros((extra, width), bf16)
                 g[place.plane_peer(k), later, :] = jnp.zeros((extra, width), bf16)
+
+            each(clear)
 
     def part(kind, gi, u):
         group = lax.rem(my_group + 1 + gi, groups)
@@ -442,7 +469,12 @@
 
             def put(i, stage, landed_here, s):
                 pl.when(i >= 2)(lambda: put_copy(i, stage, s).wait())
-                out[lax.rem(i, 2)] = acc[...].astype(bf16)
+                slot = lax.rem(i, 2)
+
+                def cast(where):
+                    out[slot, where, :] = acc[where, :].astype(bf16)
+
+                by_rows(capacity, cast)
                 pl.when(i == 0)(lambda: put_copy(i, landed_here, s).start())
                 pl.when(i > 0)(lambda: put_copy(i, stage, s).start())
 
@@ -451,7 +483,7 @@
                     put_copy(i, stage, plane).wait()
 
             def forward(s):
-                acc[...] = jnp.zeros_like(acc)
+                by_rows(capacity, lambda where: acc.__setitem__((where, slice(None)), jnp.zeros((96, width), f32)))
 
                 def step(t, carry):
                     here = pl.ds(pl.multiple_of(t * tile, tile), tile)
@@ -463,7 +495,7 @@
                 lax.fori_loop(0, tiles, step, 0)
 
             def backward(s):
-                acc[...] = jnp.zeros_like(acc)
+                by_rows(capacity, lambda where: acc.__setitem__((where, slice(None)), jnp.zeros((96, width), f32)))
 
                 def step(t, carry):
                     here = pl.ds(pl.multiple_of(t * tile, tile), tile)
@@ -480,11 +512,8 @@
                 lax.fori_loop(0, tiles, step, 0)
 
             def send_backs():
-                for j in peers:
-                    pieces(place.plane_peer(j), lambda i, where: g_copy(j, i, where).wait_send())
-                for m in peers:
-                    j = place.order(m, True)
-                    pieces(plane, lambda i, where: back_copy(j, i, where).start())
+                each(lambda k: pieces(place.plane_peer(k), lambda i, where: g_copy(k, i, where).wait_send()))
+                spread(lambda k, i, where: back_copy(k, i, where).start(), plane)
 
             def forward_step(n, carry):
                 k = taking(n)
@@ -492,7 +521,7 @@
                 @pl.when(n > 0)
                 def _():
                     x_load(k).wait()
-                    later_piece(plane, lambda: x_copy(k).wait_recv())
+                    later_piece(plane, lambda: x_copy(k, later).wait_recv())
 
                 s = place.plane_peer(k)
                 forward(s)
@@ -568,14 +597,24 @@
                     load.start()
                     load.wait()
                     _, inside = part(kind, gi, u)
-                    mine = pl.ds(pl.multiple_of((inside * 2 + core) * share, 8), share)
+                    begin = (inside * 2 + core) * share
+
+                    def total_at(where):
+                        mine = pl.ds(pl.multiple_of(begin + where.start, 32), where.size)
+                        return stage[kind, mine, :] + other[where, :]
 
                     def pass_on():
-                        sums_out[kind, gi * joint + (u - 1) % joint] = (stage[kind, mine, :] + other[...]).astype(bf16)
+                        def put(where):
+                            sums_out[kind, gi * joint + (u - 1) % joint, where, :] = total_at(where).astype(bf16)
+
+                        by_rows(share, put)
                         sum_copy(kind, gi, u).start()
 
                     def keep():
-                        own_sum[kind] = stage[kind, mine, :] + other[...]
+                        def put(where):
+                            own_sum[kind, where, :] = total_at(where)
+
+                        by_rows(share, put)
 
                     if u:
                         pass_on()
@@ -636,33 +675,32 @@
                 copy.start()
             for copy in fetch:
                 copy.wait()
-            dots = jnp.sum(back_rows[...].astype(f32) * held_rows[...].astype(f32), axis=1, keepdims=True)
-            mask = lax.broadcasted_iota(jnp.int32, (capacity, count), 0) == slots[e]
-            row_buf[0:1, :] = jnp.sum(jnp.where(mask, dots, 0.0), axis=0, keepdims=True)
+            row_buf[0:1, :] = jnp.zeros((1, count), f32)
+
+            def dot_rows(where):
+                dots = jnp.sum(back_rows[where, :].astype(f32) * held_rows[where, :].astype(f32), axis=1, keepdims=True)
+                mask = lax.broadcasted_iota(jnp.int32, (64, count), 0) + where.start == slots[e]
+                row_buf[0:1, :] += jnp.sum(jnp.where(mask, dots, 0.0), axis=0, keepdims=True)
+
+            by_rows(capacity, dot_rows, 64)
             for i in range(8):
                 own_grads[e, i : i + 1, :] = row_buf[0:1, i * lanes : (i + 1) * lanes]
             return carry
 
         lax.fori_loop(0, planes, dots_step, 0)
         own_grads_copy.start()
-        plane_gather(place, own_grads, all_grads, plane_send, plane_recv)
+        plane_gather(place, own_grads, all_grads, plane_send, plane_recv, True)
 
     def begin_slopes():
-        for k in peers:
-            pieces(plane, lambda i, where: back_copy(k, i, where).wait_send())
+        each(lambda k: pieces(plane, lambda i, where: back_copy(k, i, where).wait_send()))
         slope_copy(planes - 1, 0, first).start()
 
     def send_slopes():
-        for n in peers:
-            k = place.order(n, True)
-
-            def start(i, where):
-                if i:
-                    slope_copy(k, i, where).start()
-                else:
-                    pl.when(k != planes - 1)(lambda: slope_copy(k, i, where).start())
-
-            pieces(plane, start)
+        spread(
+            lambda k, i, where: slope_copy(k, i, where).start(),
+            plane,
+            lambda k, i: jnp.logical_or(i > 0, k != planes - 1),
+        )
 
     pl.run_scoped(
         lambda act, pre_g: (compute(act, pre_g), None)[1],
@@ -711,8 +749,7 @@
         pltpu.VMEM((planes, capacity, width), bf16),
         pltpu.VMEM((count // long, long, width), bf16),
     )
-    for copy in plane_gather(place, own_grads, all_grads, plane_send, plane_recv, False):
-        copy.wait()
+    plane_gather(place, own_grads, all_grads, plane_send, plane_recv, False)
     own_grads_copy.wait()
     column_gather_start(place, all_grads, column_send, column_recv)
 
@@ -724,12 +761,10 @@
 
     def total_start(part, planes_held):
         planes_held[plane] = part[...]
-        for k in peers:
-            total_copy(part, planes_held, total_sem, k).start()
+        each(lambda k: total_copy(part, planes_held, total_sem, k).start())
 
     def total_middle(part, planes_held, own, columns_held):
-        for k in peers:
-            total_copy(part, planes_held, total_sem, k).wait()
+        each(lambda k: total_copy(part, planes_held, total_sem, k).wait())
         own[...] = lax.fori_loop(1, planes, lambda e, held: held + planes_held[e], planes_held[0])
         columns_held[column] = own[...]
 
@@ -774,7 +809,7 @@
         ]
         for load in loads:
             load.start()
-        routed[...] = jnp.zeros_like(routed)
+        by_rows(count, lambda where: routed.__setitem__((where, slice(None)), jnp.zeros((128, width), f32)), 128)
 
         def fetch_rows(n):
             k = taking(n)
@@ -868,7 +903,11 @@
             pl.when(j < 2 * chips - 3)(lambda: part_arrived(j + 1))
             part_load(j).wait()
             kind = lax.rem(j, 2)
-            own_sum[kind] = own_sum[kind] + part[kind].astype(f32)
+
+            def put(where):
+                own_sum[kind, where, :] = own_sum[kind, where, :] + part[kind, where, :].astype(f32)
+
+            by_rows(share, put)
             return carry
 
         part_arrived(jnp.int32(0))
@@ -905,9 +944,12 @@
         return carry
 
     lax.fori_loop(0, 2 * chips - 2, sent, 0)
-    for k in peers:
-        later_piece(place.plane_peer(k), lambda: x_copy(k).wait_send())
+
+    def finish_sends(k):
+        later_piece(place.plane_peer(k), lambda: x_copy(k, later).wait_send())
         pieces(plane, lambda i, where: slope_copy(k, i, where).wait_send())
+
+    each(finish_sends)
 
 
 def result_kernel(planes, up_in, down_in, mixed_in, input_in, totals, up, down, mixed, inputs, gain, router, rows, turned, wide, sem):

time: 369 us -> 331 us (0.90); the launches traced: 376 us -> 331 us
  Pallas kernels: 362 us -> 317 us
    pallas_call x2, Pallas kernels: 352 us -> 308 us  [call(): pl.pallas_call(kernel, out_shape=[jax.ShapeDtypeStruct(shape, kind) for s...]
where the time goes in v1:
time: 331 us
  Pallas kernels  317 us (96%)
  loops' own time  12.5 us (4%)
    pallas_call x2, Pallas kernels, call(): pl.pallas_call(kernel, out_shape=[jax.ShapeDtypeStruct(shape, kind) for s...  308 us
    another operation x1, loops' own time, on_device(): lax.switch(choice[0], branches, *arrays)  12.5 us
    pallas_call x1, Pallas kernels, on_device(): pl.pallas_call(functools.partial(result_kernel, planes), out_shape=[jax.S...  9.38 us

profile of v1, /device:TPU:0, one launch (start us, length us, event | category | flops | bytes accessed | tf_op | source)
XLA Modules:
  0.0 331.4 jit_solution(17169410351728246398)
XLA Ops:
  0.6 0.0 copy-start
  0.6 48.2 %shard_map.118 = (bf16[4,384,1152]{2,1,0:T(8,128)(2,1)S(1)}, bf16[4,384,1152]{2,1,0:T(8,128)(2,1)}, bf16[4,384,1152]{2,1,0:T(8,128)(2,1)}, bf16[4,384,1152]{2,1,...) custom-call(bf16[1024,1152]{1,0:T(8,128)(2,1)} %tokens.1, ...), custom_call_target="tpu_custom_call" | custom-call | tf_op jit(solution)/shard_map/pallas_call | solution.py:984
  49.5 0.0 copy-done
  49.5 272.3 %conditional.1 = (f32[384,1152]{1,0:T(8,128)}, f32[384,1152]{1,0:T(8,128)}, bf16[1024,1152]{1,0:T(8,128)(2,1)}, f32[1024,1152]{1,0:T(8,128)}, f32[8,1152]{1,0:T(8,128)}) conditional(s32[]{:T(128)} %bitcast.2, (bf16[1,1152,3072]{2,1,0:T(8,128)(2,1)}, bf16[1,3072,1152]{2,1,0:T(8,128)(2,1)}, ...), branch_computations={%region_0.0_spmd, %region_1.0_spmd, %region_2.0_spmd, %region_3.0_... | conditional | bytes 40 | solution.py:1080
  55.4 259.8 %branch_1_fun.1 = (bf16[4,384,1152]{2,1,0:T(8,128)(2,1)}, bf16[4,384,1152]{2,1,0:T(8,128)(2,1)}, bf16[4,384,1152]{2,1,0:T(8,128)(2,1)}, bf16[4,384,1152]{2,1,0:T...) custom-call(bf16[1,1152,3072]{2,1,0:T(8,128)(2,1)} %get-tuple-elemen, ...), custom_call_target="tpu_custom_call" | custom-call | tf_op jit(solution)/shard_map/cond/branch_1_fun/pallas_call | solution.py:984
  321.7 9.4 %shard_map.119 = (f32[1,1152,384]{2,1,0:T(8,128)}, f32[1,384,1152]{2,1,0:T(8,128)}, bf16[1024,1152]{1,0:T(8,128)(2,1)}, f32[1024,1152]{1,0:T(8,128)}, f32[1152]{0:T(1024)}, /*index=5*/f32[4,1152]{1,0:T(4,128)}) custom-call(f32[384,1152]{1,0:T(8,128)} %get-tuple-element.306.up_in, f32[384,1152]{1,0:T(8,128)} %get-tuple-element.307.down_in, ...), custom_call_target="tpu_custom_call" | custom-call | tf_op jit(solution)/shard_map/pallas_call | solution.py:1082
Async XLA Ops:
  0.6 48.8 %copy-start = (f32[1152]{0:T(1024)S(1)}, f32[1152]{0:T(1024)}, u32[]{:S(2)}) copy-start(f32[1152]{0:T(1024)} %gain_in.1) | copy-start | bytes 13828
